TPU v7x, 128 devices: a whole 4x4x4 slice. The times are simulated.
128 devices in a mesh: ctx: 16 (over z, x_lo, core), tp: 4 (over y), dp: 2 (over x_hi).
Axes of the slice: x: 4 (x_hi: 2, x_lo: 2; x = x_hi * 2 + x_lo), y: 4, z: 4, core: 2. Of those that a mesh axis runs over, the one named last changes fastest.
Arguments:
- queries: bfloat16 [16384, 2048], P(('dp', 'ctx'), 'tp'), parts along dimension 0, may hold values from -6 to 6
- keys: bfloat16 [16384, 512], P(('dp', 'ctx'), 'tp'), parts along dimension 0, may hold values from -6 to 6
- values: bfloat16 [16384, 512], P(('dp', 'ctx'), 'tp'), parts along dimension 0, may hold values from -6 to 6
- outputs: bfloat16 [16384, 2048], P(('dp', 'ctx'), 'tp'), parts along dimension 0, may hold values from -4 to 4
- out_grads: bfloat16 [16384, 2048], P(('dp', 'ctx'), 'tp'), parts along dimension 0, may hold values from -6 to 6
- log_norms: float32 [16, 16384], P('tp', ('dp', 'ctx')), parts along dimension 1, may hold values from 3 to 6
- stretch_order: int32 [64], P('dp'), parts along dimension 0, may hold values from 0 to 31, each once
Outputs:
- grad_queries: bfloat16 [16384, 2048], P(('dp', 'ctx'), 'tp'), parts along dimension 0
- grad_keys: bfloat16 [16384, 512], P(('dp', 'ctx'), 'tp'), parts along dimension 0
- grad_values: bfloat16 [16384, 512], P(('dp', 'ctx'), 'tp'), parts along dimension 0
There are 2 independent parts, one for each index of `dp`. A program takes and returns all parts, laid end to end along the dimension named above; each array names one. Nothing has to cross between parts.
Inputs may be any that keep to these rules, and one draw needn't show every extreme that they name: stretch_order is a permutation of the 32 sequence blocks of 256 tokens.
All inputs are finite; a program needn't handle non-finite values.
Results may differ from a plain program's by a relative error of at most 0.023.
Values may be sent and summed in bfloat16 or wider, within the bound.
A program may use at most 64 MiB of HBM per device.

v0:
```python
import jax
import jax.numpy as jnp
from jax import lax
from jax.sharding import PartitionSpec as P

QH = 16
KVH = 4
HD = 128


def positions_of(stretch_order, first_stretch, count, stretch_size):
    offsets = jnp.arange(count, dtype=jnp.int32)
    stretch_ids = first_stretch + offsets // stretch_size
    return jnp.take(stretch_order, stretch_ids) * stretch_size + offsets % stretch_size


def tile_grads(
    query_heads, grad_heads, norm_heads, delta_rows, query_pos, key_block, value_block, key_pos
):
    block_rows = key_block.shape[0]
    kv_local = query_heads.shape[1]
    score_scale = HD ** (-0.5)
    key_heads = key_block.reshape(block_rows, kv_local, HD)
    value_heads = value_block.reshape(block_rows, kv_local, HD)
    scores = (
        jnp.einsum("rhgd,chd->hgrc", query_heads, key_heads, preferred_element_type=jnp.float32)
        * score_scale
    )
    allowed = key_pos[None, :] <= query_pos[:, None]
    probs = jnp.where(
        allowed[None, None], jnp.exp(scores - norm_heads[:, :, :, None]), jnp.float32(0.0)
    )
    probs_low = probs.astype(jnp.bfloat16)
    grad_value = jnp.einsum(
        "hgrc,rhgd->chd", probs_low, grad_heads, preferred_element_type=jnp.float32
    )
    grad_probs = jnp.einsum(
        "rhgd,chd->hgrc", grad_heads, value_heads, preferred_element_type=jnp.float32
    )
    grad_scores = (score_scale * probs * (grad_probs - delta_rows[:, :, :, None])).astype(
        jnp.bfloat16
    )
    grad_query = jnp.einsum(
        "hgrc,chd->rhgd", grad_scores, key_heads, preferred_element_type=jnp.float32
    )
    grad_key = jnp.einsum(
        "hgrc,rhgd->chd", grad_scores, query_heads, preferred_element_type=jnp.float32
    )
    return (
        grad_query,
        grad_key.reshape(block_rows, kv_local * HD),
        grad_value.reshape(block_rows, kv_local * HD),
    )


def shards(queries, keys, values, outputs, out_grads, log_norms, stretch_order):
    local_rows = queries.shape[0]
    stretch_size = local_rows // 2
    kv_local = keys.shape[1] // HD
    width = kv_local * HD
    group_size = QH // KVH
    my_index = lax.axis_index("ctx")
    query_heads = queries.reshape(local_rows, kv_local, group_size, HD)
    grad_heads = out_grads.reshape(local_rows, kv_local, group_size, HD)
    output_heads = outputs.reshape(local_rows, kv_local, group_size, HD)
    delta_rows = jnp.sum(
        grad_heads.astype(jnp.float32) * output_heads.astype(jnp.float32), axis=3
    ).transpose(1, 2, 0)
    norm_heads = log_norms.reshape(kv_local, group_size, local_rows)
    query_pos = positions_of(stretch_order, my_index * 2, local_rows, stretch_size)

    def attend_block(key_block, value_block, key_pos):
        return tile_grads(
            query_heads,
            grad_heads,
            norm_heads,
            delta_rows,
            query_pos,
            key_block,
            value_block,
            key_pos,
        )

    grad_start = jnp.zeros((local_rows, kv_local, group_size, HD), jnp.float32)
    key_all, value_all = (
        lax.all_gather(keys, "ctx", axis=0, tiled=True),
        lax.all_gather(values, "ctx", axis=0, tiled=True),
    )
    total_rows = key_all.shape[0]
    block_size = 2 * local_rows
    all_pos = positions_of(stretch_order, jnp.int32(0), total_rows, stretch_size)

    def visit(block_index, state_tuple):
        grad_query, grad_term = state_tuple
        start_row = block_index * block_size
        key_block = lax.dynamic_slice_in_dim(key_all, start_row, block_size, 0)
        value_block = lax.dynamic_slice_in_dim(value_all, start_row, block_size, 0)
        key_pos = lax.dynamic_slice_in_dim(all_pos, start_row, block_size, 0)
        query_add, grad_key, grad_value = attend_block(key_block, value_block, key_pos)
        grad_term = lax.dynamic_update_slice_in_dim(
            grad_term, jnp.concatenate([grad_key, grad_value], axis=1), start_row, 0
        )
        return (grad_query + query_add, grad_term)

    term_start = jnp.zeros((total_rows, 2 * width), jnp.float32)
    grad_query, grad_term = lax.fori_loop(
        0, total_rows // block_size, visit, (grad_start, term_start)
    )
    summed = lax.psum_scatter(
        grad_term.astype(jnp.bfloat16), "ctx", scatter_dimension=0, tiled=True
    ).astype(jnp.float32)
    grad_queries = grad_query.reshape(local_rows, kv_local * group_size * HD).astype(jnp.bfloat16)
    grad_keys = summed[:, :width].astype(jnp.bfloat16)
    grad_values = summed[:, width:].astype(jnp.bfloat16)
    return (grad_queries, grad_keys, grad_values)


def solution(mesh):
    return jax.shard_map(
        shards,
        mesh=mesh,
        in_specs=(
            P(("dp", "ctx"), "tp"),
            P(("dp", "ctx"), "tp"),
            P(("dp", "ctx"), "tp"),
            P(("dp", "ctx"), "tp"),
            P(("dp", "ctx"), "tp"),
            P("tp", ("dp", "ctx")),
            P("dp"),
        ),
        out_specs=(P(("dp", "ctx"), "tp"), P(("dp", "ctx"), "tp"), P(("dp", "ctx"), "tp")),
        check_vma=False,
    )
```

profile of v0, /device:TPU:0, one launch (start us, length us, event | category | flops | bytes accessed | tf_op | source)
XLA Modules:
  0.0 266.6 jit_solution(16968993877155882788)
XLA Ops:
  16.2 4.3 %compare_select_fusion.9 = s32[512,1]{0,1:T(1,128)S(1)} fusion(s32[]{:T(128)} %bitcast.25, s32[]{:T(128)} %bitcast.26, s32[]{:T(128)} %bitcast.27, s32[]{:T(128)} %bitcast.28, s32[]{:T(128)} %bitcast.29, s32[]{:T(128)} %bitcast.31, s32[]{:T(128)} %bitcast.30, s32[]{:T(128)S(6)} %mul.57), kind=kLoop, calls=%fused_computation.115 | loop fusion | flops 12288 | bytes 2080 | tf_op jit(solution)/shard_map/jit(_take)/gather | solution.py:14
  21.5 15.8 %fusion.47 = s32[512]{0:T(512)S(1)} fusion(pred[512]{0:T(512)(128)(4,1)S(1)} %get-tuple-element.282, pred[512]{0:T(512)(128)(4,1)S(1)} %get-tuple-element.283, pred[512]{0:T(512)(128)(4,1)S(1)} %get-tuple-element.284, pred[512]{0:T(512)(128)(4,1)S(1)} %get-tuple-element.285, pred[512]{0:T(512)(128)(4,1)S(1)} %get-tuple-element.286, ...), kind=kLoop, calls=%fused_computation.135 | loop fusion | flops 24064 | bytes 17000 | tf_op jit(solution)/shard_map/add | solution.py:14
  37.3 4.3 %compare_select_fusion.1 = s32[8192,1]{0,1:T(1,128)S(1)} fusion(s32[]{:T(128)} %bitcast.25, s32[]{:T(128)} %bitcast.26, s32[]{:T(128)} %bitcast.27, s32[]{:T(128)} %bitcast.28, s32[]{:T(128)} %bitcast.29, s32[]{:T(128)} %bitcast.31, s32[]{:T(128)} %bitcast.30), kind=kLoop, calls=%fused_computation.61 | loop fusion | flops 188416 | bytes 32796 | tf_op jit(solution)/shard_map/jit(_take)/gather | solution.py:14
  41.6 15.9 %fusion.36 = s32[8192]{0:T(1024)S(1)} fusion(pred[8192]{0:T(1024)(128)(4,1)S(1)} %compare_reduce_fusion, pred[8192]{0:T(1024)(128)(4,1)S(1)} %compare_reduce_fusion.1, pred[8192]{0:T(1024)(128)(4,1)S(1)} %compare_reduce_fusion.2, pred[8192]{0:T(1024)(128)(4,1)S(1)} %compare_reduce_fusion.3, pred[8192]{0:T(1024)(128)(4,1)S(1)} %compare_reduce_fusion.4, ...), kind=kLoop, calls=%fused_computation.82 | loop fusion | flops 376832 | bytes 270436 | tf_op jit(solution)/shard_map/add | solution.py:14
  57.5 24.7 %all-gather.5.cloned.1.call-done = bf16[8192,128]{1,0:T(8,128)(2,1)} async-done(((bf16[512,128]{1,0:T(8,128)(2,1)}), bf16[8192,128]{1,0:T(8,128)(2,1)}) %all-gather.5.cloned.1.call-update) | async-done | bytes 2097168 | tf_op jit(solution)/shard_map/all_gather | solution.py:87
  82.2 2.2 broadcast_in_dim.55.clone
  84.4 104.4 %while.16 = (s32[]{:T(128)}, f32[512,1,4,128]{0,3,2,1:T(8,128)S(1)}, bf16[8192,256]{1,0:T(8,128)(2,1)}, bf16[8192,128]{1,0:T(8,128)(2,1)}, s32[8192]{0:T(1024)S(...) while((s32[]{:T(128)}, ...), condition=%wide.region_2.3_spmd.clone, body=%wide.region_1.2_spmd.clone.sunk | while | flops 2709520384 | bytes 48011488 | solution.py:106
  84.8 2.2 fusion.82
  87.0 2.0 fusion.85
  89.0 4.1 %fusion.83 = bf16[4,512,1024]{1,2,0:T(8,128)(2,1)S(1)} fusion(f32[1024,512,4]{1,0,2:T(8,128)S(1)} %fusion.82, f32[4,512]{1,0:T(4,128)S(1)} %bitcast.152, f32[4,512]{1,0:T(4,128)S(1)} %get-tuple-element.410, pred[512,1024]{0,1:T(8,128)(4,1)S(1)} %broadcast_compare_fusion.2, bf16[512,1,4,128]{0,3,2,1:T(8,128)(2,1)S(1)} %get-tuple-element.412, ...), kind=kOutput, calls=%fused_computation.8.clone.1 | convolution fusion | flops 551550976 | bytes 13910020 | tf_op jit(solution)/shard_map/while/body/eval_jaxpr/rhgd,chd->hgrc/dot_general | solution.py:37
  97.8 2.2 fusion.82
  100.0 2.0 fusion.85
  102.0 4.1 %fusion.83 = bf16[4,512,1024]{1,2,0:T(8,128)(2,1)S(1)} fusion(f32[1024,512,4]{1,0,2:T(8,128)S(1)} %fusion.82, f32[4,512]{1,0:T(4,128)S(1)} %bitcast.152, f32[4,512]{1,0:T(4,128)S(1)} %get-tuple-element.410, pred[512,1024]{0,1:T(8,128)(4,1)S(1)} %broadcast_compare_fusion.2, bf16[512,1,4,128]{0,3,2,1:T(8,128)(2,1)S(1)} %get-tuple-element.412, ...), kind=kOutput, calls=%fused_computation.8.clone.1 | convolution fusion | flops 551550976 | bytes 13910020 | tf_op jit(solution)/shard_map/while/body/eval_jaxpr/rhgd,chd->hgrc/dot_general | solution.py:37
  110.9 2.2 fusion.82
  113.1 2.0 fusion.85
  115.1 4.1 %fusion.83 = bf16[4,512,1024]{1,2,0:T(8,128)(2,1)S(1)} fusion(f32[1024,512,4]{1,0,2:T(8,128)S(1)} %fusion.82, f32[4,512]{1,0:T(4,128)S(1)} %bitcast.152, f32[4,512]{1,0:T(4,128)S(1)} %get-tuple-element.410, pred[512,1024]{0,1:T(8,128)(4,1)S(1)} %broadcast_compare_fusion.2, bf16[512,1,4,128]{0,3,2,1:T(8,128)(2,1)S(1)} %get-tuple-element.412, ...), kind=kOutput, calls=%fused_computation.8.clone.1 | convolution fusion | flops 551550976 | bytes 13910020 | tf_op jit(solution)/shard_map/while/body/eval_jaxpr/rhgd,chd->hgrc/dot_general | solution.py:37
  123.9 2.2 fusion.82
  126.1 2.0 fusion.85
  128.1 4.1 %fusion.83 = bf16[4,512,1024]{1,2,0:T(8,128)(2,1)S(1)} fusion(f32[1024,512,4]{1,0,2:T(8,128)S(1)} %fusion.82, f32[4,512]{1,0:T(4,128)S(1)} %bitcast.152, f32[4,512]{1,0:T(4,128)S(1)} %get-tuple-element.410, pred[512,1024]{0,1:T(8,128)(4,1)S(1)} %broadcast_compare_fusion.2, bf16[512,1,4,128]{0,3,2,1:T(8,128)(2,1)S(1)} %get-tuple-element.412, ...), kind=kOutput, calls=%fused_computation.8.clone.1 | convolution fusion | flops 551550976 | bytes 13910020 | tf_op jit(solution)/shard_map/while/body/eval_jaxpr/rhgd,chd->hgrc/dot_general | solution.py:37
  137.0 2.2 fusion.82
  139.2 2.0 fusion.85
  141.2 4.1 %fusion.83 = bf16[4,512,1024]{1,2,0:T(8,128)(2,1)S(1)} fusion(f32[1024,512,4]{1,0,2:T(8,128)S(1)} %fusion.82, f32[4,512]{1,0:T(4,128)S(1)} %bitcast.152, f32[4,512]{1,0:T(4,128)S(1)} %get-tuple-element.410, pred[512,1024]{0,1:T(8,128)(4,1)S(1)} %broadcast_compare_fusion.2, bf16[512,1,4,128]{0,3,2,1:T(8,128)(2,1)S(1)} %get-tuple-element.412, ...), kind=kOutput, calls=%fused_computation.8.clone.1 | convolution fusion | flops 551550976 | bytes 13910020 | tf_op jit(solution)/shard_map/while/body/eval_jaxpr/rhgd,chd->hgrc/dot_general | solution.py:37
  150.0 2.2 fusion.82
  152.2 2.0 fusion.85
  154.2 4.1 %fusion.83 = bf16[4,512,1024]{1,2,0:T(8,128)(2,1)S(1)} fusion(f32[1024,512,4]{1,0,2:T(8,128)S(1)} %fusion.82, f32[4,512]{1,0:T(4,128)S(1)} %bitcast.152, f32[4,512]{1,0:T(4,128)S(1)} %get-tuple-element.410, pred[512,1024]{0,1:T(8,128)(4,1)S(1)} %broadcast_compare_fusion.2, bf16[512,1,4,128]{0,3,2,1:T(8,128)(2,1)S(1)} %get-tuple-element.412, ...), kind=kOutput, calls=%fused_computation.8.clone.1 | convolution fusion | flops 551550976 | bytes 13910020 | tf_op jit(solution)/shard_map/while/body/eval_jaxpr/rhgd,chd->hgrc/dot_general | solution.py:37
  163.1 2.2 fusion.82
  165.3 2.0 fusion.85
  167.3 4.1 %fusion.83 = bf16[4,512,1024]{1,2,0:T(8,128)(2,1)S(1)} fusion(f32[1024,512,4]{1,0,2:T(8,128)S(1)} %fusion.82, f32[4,512]{1,0:T(4,128)S(1)} %bitcast.152, f32[4,512]{1,0:T(4,128)S(1)} %get-tuple-element.410, pred[512,1024]{0,1:T(8,128)(4,1)S(1)} %broadcast_compare_fusion.2, bf16[512,1,4,128]{0,3,2,1:T(8,128)(2,1)S(1)} %get-tuple-element.412, ...), kind=kOutput, calls=%fused_computation.8.clone.1 | convolution fusion | flops 551550976 | bytes 13910020 | tf_op jit(solution)/shard_map/while/body/eval_jaxpr/rhgd,chd->hgrc/dot_general | solution.py:37
  176.1 2.2 fusion.82
  178.3 2.0 fusion.85
  180.3 4.1 %fusion.83 = bf16[4,512,1024]{1,2,0:T(8,128)(2,1)S(1)} fusion(f32[1024,512,4]{1,0,2:T(8,128)S(1)} %fusion.82, f32[4,512]{1,0:T(4,128)S(1)} %bitcast.152, f32[4,512]{1,0:T(4,128)S(1)} %get-tuple-element.410, pred[512,1024]{0,1:T(8,128)(4,1)S(1)} %broadcast_compare_fusion.2, bf16[512,1,4,128]{0,3,2,1:T(8,128)(2,1)S(1)} %get-tuple-element.412, ...), kind=kOutput, calls=%fused_computation.8.clone.1 | convolution fusion | flops 551550976 | bytes 13910020 | tf_op jit(solution)/shard_map/while/body/eval_jaxpr/rhgd,chd->hgrc/dot_general | solution.py:37
  189.9 68.5 %reduce-scatter.2.cloned.1.call-done = bf16[512,256]{1,0:T(8,128)(2,1)} async-done(((bf16[8192,256]{1,0:T(8,128)(2,1)}), bf16[512,256]{1,0:T(8,128)(2,1)}) %reduce-scatter.2.cloned.1.call-update) | async-done | bytes 262160 | tf_op jit(solution)/shard_map/reduce_scatter | solution.py:109
  (115 shorter events, 50.2 us)
Async XLA Ops:
  7.2 13.3 %copy-start = (s32[32]{0:T(128)S(1)}, s32[32]{0:T(128)}, u32[]{:S(2)}) copy-start(s32[32]{0:T(128)} %param.15) | copy-start | bytes 388
  7.2 50.3 %all-gather.3.cloned.1.call-start = ((), (), s32[]{:S(2)}) async-start(), calls=%async_computation.1 | async-start | bytes 2228224 | tf_op jit(solution)/shard_map/all_gather | solution.py:86
  7.9 74.3 %all-gather.5.cloned.1.call-start = ((), (), s32[]{:S(2)}) async-start(), calls=%async_computation.2 | async-start | bytes 2228224 | tf_op jit(solution)/shard_map/all_gather | solution.py:87
  8.7 249.7 %reduce-scatter.2.cloned.1.call-start = ((), (), s32[]{:S(2)}) async-start(), calls=%async_computation.3 | async-start | bytes 4456448 | tf_op jit(solution)/shard_map/reduce_scatter | solution.py:109
  11.2 73.2 %copy-start.1 = (f32[4,512]{1,0:T(4,128)S(1)}, f32[4,512]{1,0:T(4,128)}, u32[]{:S(2)}) copy-start(f32[4,512]{1,0:T(4,128)} %param.14) | copy-start | bytes 24580
Sparse Core Ops, SparseCore 0:
  9.7 36.7 all-gather.2
  48.2 33.9 all-gather.4
  188.9 69.3 reduce-scatter.1
where the time goes:
time: 269 us; the launch traced here: 267 us
  waiting for transfers between devices  94.6 us (35%)
  matrix products  92.4 us (34%)
  other arithmetic  45.6 us (17%)
  local copies, waits for them, and re-layouts  19.6 us (7%)
  between operations  13.9 us (5%)
    reduce_scatter x1, waiting for transfers between devices, shards(): lax.psum_scatter(grad_term.astype(jnp.bfloat16), 'ctx', scatter_dimension...  68.5 us
    dot_general x8, matrix products, tile_grads(): jnp.einsum('rhgd,chd->hgrc', grad_heads, value_heads, preferred_element_t...  32.9 us
    add x2, other arithmetic, positions_of(): jnp.take(stretch_order, stretch_ids) * stretch_size + offsets % stretch_size  31.7 us
    all_gather x1, waiting for transfers between devices, shards(): lax.all_gather(values, 'ctx', axis=0, tiled=True)  24.7 us
    dot_general x8, matrix products, tile_grads(): jnp.einsum('rhgd,chd->hgrc', query_heads, key_heads, preferred_element_ty...  17.5 us
    dot_general x8, matrix products, tile_grads(): jnp.einsum('hgrc,rhgd->chd', probs_low, grad_heads, preferred_element_typ...  16 us
    dot_general x8, matrix products, tile_grads(): jnp.einsum('hgrc,chd->rhgd', grad_scores, key_heads, preferred_element_ty...  14.2 us
    dot_general x8, matrix products, tile_grads(): jnp.einsum('hgrc,rhgd->chd', grad_scores, query_heads, preferred_element_...  11.8 us
  transfers between devices with their start and end apart: 3, of which 2 were waited for; matrix products, arithmetic and copies ran while one was open for 19% of the time, Pallas kernels for 0%

commit v1 on v0

v1 whole, which is shorter than its diff:
```python
import functools

import jax
import jax.numpy as jnp
from jax import lax
from jax.experimental import pallas as pl
from jax.experimental.pallas import tpu as pltpu
from jax.sharding import PartitionSpec as P

HD = 128
HEADS = 4
STRETCH = 256
ROWS = 512
KEYS = 1024
F32 = jnp.float32
BF16 = jnp.bfloat16
LOG2E = 1.4426950408889634
SCALE = HD ** (-0.5)
HIDDEN = -1e30


def dot(a, b, ca=1, cb=0):
    return lax.dot_general(a, b, (((ca,), (cb,)), ((), ())), preferred_element_type=F32)


def prepare(q_in, do_in, o_in, norm_in, qh, doh, qt, dot_, nb, dl, dqa):
    norm = norm_in[...] * LOG2E
    norm_cols = jnp.concatenate([norm, norm], axis=0).T
    for h in range(HEADS):
        rows = slice(h * ROWS, (h + 1) * ROWS)
        cols = slice(h * HD, (h + 1) * HD)
        q = q_in[:, cols]
        do = do_in[:, cols]
        qh[rows, :] = q
        doh[rows, :] = do
        qt[:, rows] = q.T
        dot_[:, rows] = do.T
        delta = jnp.sum(do.astype(F32) * o_in[:, cols].astype(F32), axis=1, keepdims=True)
        nb[rows, :] = jnp.broadcast_to(norm_cols[:, h : h + 1], (ROWS, HD))
        dl[rows, :] = jnp.broadcast_to(delta, (ROWS, HD))
    dqa[...] = jnp.zeros_like(dqa)


def step(k, v, kpos, qpos, qh, doh, qt, dot_, nb, dl, dqa, ps, dss):
    sub = 256
    for j in range(HEADS * ROWS // sub):
        rows = slice(j * sub, (j + 1) * sub)
        s = dot(qh[rows, :], k, 1, 1)
        dp = dot(doh[rows, :], v, 1, 1)
        seen = kpos <= qpos[j % 2]
        p = jnp.exp2(jnp.where(seen, s * (SCALE * LOG2E) - nb[rows, 0:1], HIDDEN))
        ds = (p * (dp - dl[rows, 0:1])).astype(BF16)
        ps[rows, :] = p.astype(BF16)
        dss[rows, :] = ds
        dqa[rows, :] += dot(ds, k)
    return dot(qt[...], dss[...]), dot(dot_[...], ps[...])


def kernel(q_in, do_in, o_in, norm_in, k_all, v_all, kpos_in, qpos_in, dq_out, term_out,
           qh, doh, qt, dot_, nb, dl, dqa, ps, dss):
    prepare(q_in, do_in, o_in, norm_in, qh, doh, qt, dot_, nb, dl, dqa)

    def body(i, _):
        ks = pl.ds(pl.multiple_of(i * KEYS, KEYS), KEYS)
        qpos = [qpos_in[0:STRETCH, 0:1], qpos_in[STRETCH:, 0:1]]
        dk, dv = step(k_all[ks, :], v_all[ks, :], kpos_in[0:1, ks], qpos,
                      qh, doh, qt, dot_, nb, dl, dqa, ps, dss)
        term_out[ks, 0:HD] = (dk * SCALE).astype(BF16).T
        term_out[ks, HD:] = dv.astype(BF16).T
        return 0

    lax.fori_loop(0, k_all.shape[0] // KEYS, body, 0)
    for h in range(HEADS):
        dq_out[:, h * HD : (h + 1) * HD] = (dqa[h * ROWS : (h + 1) * ROWS, :] * SCALE).astype(BF16)


def shards(queries, keys, values, outputs, out_grads, log_norms, stretch_order):
    me = lax.axis_index("ctx")
    key_all = lax.all_gather(keys, "ctx", axis=0, tiled=True)
    value_all = lax.all_gather(values, "ctx", axis=0, tiled=True)
    total = key_all.shape[0]
    pos = (stretch_order[:, None] * STRETCH + jnp.arange(STRETCH, dtype=jnp.int32)).reshape(-1)
    kpos = jnp.broadcast_to(pos[None, :], (8, total))
    qpos = lax.dynamic_slice_in_dim(pos, me * ROWS, ROWS, 0)
    qpos = jnp.broadcast_to(qpos[:, None], (ROWS, HD))
    rows = HEADS * ROWS
    vmem = pl.BlockSpec(memory_space=pltpu.VMEM)
    dq, term = pl.pallas_call(
        kernel,
        out_shape=[
            jax.ShapeDtypeStruct((ROWS, HEADS * HD), BF16),
            jax.ShapeDtypeStruct((total, 2 * HD), BF16),
        ],
        in_specs=[vmem] * 8,
        out_specs=[vmem] * 2,
        scratch_shapes=[
            pltpu.VMEM((rows, HD), BF16),
            pltpu.VMEM((rows, HD), BF16),
            pltpu.VMEM((HD, rows), BF16),
            pltpu.VMEM((HD, rows), BF16),
            pltpu.VMEM((rows, HD), F32),
            pltpu.VMEM((rows, HD), F32),
            pltpu.VMEM((rows, HD), F32),
            pltpu.VMEM((rows, KEYS), BF16),
            pltpu.VMEM((rows, KEYS), BF16),
        ],
        compiler_params=pltpu.CompilerParams(vmem_limit_bytes=58 * 2**20),
    )(queries, out_grads, outputs, log_norms, key_all, value_all, kpos, qpos)
    summed = lax.psum_scatter(term, "ctx", scatter_dimension=0, tiled=True)
    return dq, summed[:, :HD], summed[:, HD:]


def solution(mesh):
    return jax.shard_map(
        shards,
        mesh=mesh,
        in_specs=(
            P(("dp", "ctx"), "tp"),
            P(("dp", "ctx"), "tp"),
            P(("dp", "ctx"), "tp"),
            P(("dp", "ctx"), "tp"),
            P(("dp", "ctx"), "tp"),
            P("tp", ("dp", "ctx")),
            P("dp"),
        ),
        out_specs=(P(("dp", "ctx"), "tp"), P(("dp", "ctx"), "tp"), P(("dp", "ctx"), "tp")),
        check_vma=False,
    )
```

time: 269 us -> 210 us (0.78)
  matrix products: 92.4 us -> 0 us
  waiting for transfers between devices: 94.6 us -> 144 us
  Pallas kernels: 0 us -> 47.7 us
  other arithmetic: 45.6 us -> 0.73 us
  local copies, waits for them, and re-layouts: 19.6 us -> 3.36 us
    dot_general x40 -> x0, matrix products: 92.4 us -> none  [the longest x8 32.9 us: tile_grads(): jnp.einsum('rhgd,chd->hgrc', grad_heads, value_heads, preferred_element_t...]
    all_gather x2, waiting for transfers between devices: 24.7 us -> 72.6 us  [the longest x1 36.9 us: shards(): key_all = lax.all_gather(keys, 'ctx', axis=0, tiled=True)]
    pallas_call x0 -> x1, Pallas kernels: none -> 47.7 us  [shards(): pl.pallas_call(kernel, out_shape=[jax.ShapeDtypeStruct((ROWS, HEADS * HD)...]
    add x2 -> x0, other arithmetic: 31.7 us -> none  [positions_of(): jnp.take(stretch_order, stretch_ids) * stretch_size + offsets % stretch_size]
    gather x40 -> x0, other arithmetic: 10.4 us -> none  [positions_of(): jnp.take(stretch_order, stretch_ids) * stretch_size + offsets % stretch_size]
    dynamic_update_slice x16 -> x0, local copies, waits for them, and re-layouts: 8.39 us -> none  [visit(): lax.dynamic_update_slice_in_dim(grad_term, jnp.concatenate([grad_key, gra...]
    le x8 -> x0, other arithmetic: 2.89 us -> none  [tile_grads(): allowed = key_pos[None, :] <= query_pos[:, None]]
  transfers between devices with their start and end apart: 3 -> 3, of which waited for: 2 -> 3; matrix products, arithmetic and copies ran while one was open for 19% -> 0% of each run, Pallas kernels for 0% -> 0%
where the time goes in v1:
time: 210 us
  waiting for transfers between devices  144 us (69%)
  Pallas kernels  47.7 us (23%)
  between operations  13.8 us (7%)
  local copies, waits for them, and re-layouts  3.36 us (2%)
    reduce_scatter x1, waiting for transfers between devices, shards(): summed = lax.psum_scatter(term, 'ctx', scatter_dimension=0, tiled=True)  70.2 us
    pallas_call x1, Pallas kernels, shards(): pl.pallas_call(kernel, out_shape=[jax.ShapeDtypeStruct((ROWS, HEADS * HD)...  47.7 us
    all_gather x1, waiting for transfers between devices, shards(): key_all = lax.all_gather(keys, 'ctx', axis=0, tiled=True)  36.9 us
    all_gather x1, waiting for transfers between devices, shards(): value_all = lax.all_gather(values, 'ctx', axis=0, tiled=True)  35.7 us
  transfers between devices with their start and end apart: 3, of which 3 were waited for; matrix products, arithmetic and copies ran while one was open for 0% of the time, Pallas kernels for 0%

profile of v1, /device:TPU:0, one launch (start us, length us, event | category | flops | bytes accessed | tf_op | source)
XLA Modules:
  0.0 209.9 jit_solution(11389978828092874544)
XLA Ops:
  7.2 0.0 all-gather.3.cloned.1.call-start
  7.2 0.7 all-gather.3.cloned.1.call-update
  7.9 0.0 all-gather.5.cloned.1.call-start
  7.9 0.7 all-gather.5.cloned.1.call-update
  8.6 0.0 reduce-scatter.2.cloned.1.call-start
  8.7 0.7 broadcast_multiply_fusion
  9.4 0.1 add_bitcast_fusion
  9.5 0.1 dynamic_slice.3
  9.5 36.9 %all-gather.3.cloned.1.call-done.k_all = bf16[8192,128]{1,0:T(8,128)(2,1)} async-done(((bf16[512,128]{1,0:T(8,128)(2,1)}), bf16[8192,128]{1,0:T(8,128)(2,1)}) %all-gather.3.cloned.1.call-update) | async-done | bytes 2097168 | tf_op jit(solution)/shard_map/all_gather | solution.py:79
  46.4 35.7 %all-gather.5.cloned.1.call-done.v_all = bf16[8192,128]{1,0:T(8,128)(2,1)} async-done(((bf16[512,128]{1,0:T(8,128)(2,1)}), bf16[8192,128]{1,0:T(8,128)(2,1)}) %all-gather.5.cloned.1.call-update) | async-done | bytes 2097168 | tf_op jit(solution)/shard_map/all_gather | solution.py:80
  82.2 0.7 broadcast_in_dim.4.kpos_in
  82.9 0.8 broadcast_in_dim.5.qpos_in
  83.7 47.7 %shard_map.94 = (bf16[512,512]{1,0:T(8,128)(2,1)}, bf16[8192,256]{1,0:T(8,128)(2,1)}) custom-call(bf16[512,512]{1,0:T(8,128)(2,1)} %q_in.1, bf16[512,512]{1,0:T(8,128)(2,1)} %do_in.1, bf16[512,512]{1,0:T(8,128)(2,1)} %o_in.1, f32[4,512]{1,0:T(4,128)} %norm_in.1, bf16[8192,128]{1,0:T(8,128)(2,1)} %all-gather.3.cloned.1.call-done.k_all, ...), custom_call_target="tpu_custom_call" | custom-call | tf_op jit(solution)/shard_map/pallas_call | solution.py:88
  131.5 0.0 reduce-scatter.2.cloned.1.call-update
  131.5 70.2 %reduce-scatter.2.cloned.1.call-done = bf16[512,256]{1,0:T(8,128)(2,1)} async-done(((bf16[8192,256]{1,0:T(8,128)(2,1)}), bf16[512,256]{1,0:T(8,128)(2,1)}) %reduce-scatter.2.cloned.1.call-update) | async-done | bytes 262160 | tf_op jit(solution)/shard_map/reduce_scatter | solution.py:109
  201.7 1.7 fusion
  (1 shorter events, 0.0 us)
Async XLA Ops:
  7.2 39.2 %all-gather.3.cloned.1.call-start = ((), (), s32[]{:S(2)}) async-start(), calls=%async_computation.1 | async-start | bytes 2228224 | tf_op jit(solution)/shard_map/all_gather | solution.py:79
  7.9 74.3 %all-gather.5.cloned.1.call-start = ((), (), s32[]{:S(2)}) async-start(), calls=%async_computation.2 | async-start | bytes 2228224 | tf_op jit(solution)/shard_map/all_gather | solution.py:80
  8.6 193.0 %reduce-scatter.2.cloned.1.call-start = ((), (), s32[]{:S(2)}) async-start(), calls=%async_computation.3 | async-start | bytes 4456448 | tf_op jit(solution)/shard_map/reduce_scatter | solution.py:109
Sparse Core Ops, SparseCore 0:
  9.7 36.6 all-gather.2
  48.1 33.9 all-gather.4
  131.6 70.0 reduce-scatter.1

commit v2 on v1

v2 whole, which is shorter than its diff:
```python
import jax
import jax.numpy as jnp
from jax import lax
from jax.experimental import pallas as pl
from jax.experimental.pallas import tpu as pltpu
from jax.sharding import PartitionSpec as P

HD = 128
HEADS = 4
STRETCH = 256
ROWS = 512
KEYS = 1024
SUB = 256
SLOTS = 8
F32 = jnp.float32
BF16 = jnp.bfloat16
LOG2E = 1.4426950408889634
SCALE = HD ** (-0.5)
HIDDEN = -1e30
LO = pl.ds(0, ROWS)
HI = pl.ds(ROWS, ROWS)

S_O, S_PM, S_PM_SIB, S_XPM, S_XZ, S_XPM_SIB, S_XANDZ_SIB, S_XANDZ = range(SLOTS)


def dot(a, b, ca=1, cb=0):
    return lax.dot_general(a, b, (((ca,), (cb,)), ((), ())), preferred_element_type=F32)


def kernel(order, q_in, do_in, o_in, norm_in, k_in, v_in, dq_out, dk_out, dv_out,
           qh, doh, qt, dot_, nb, dl, dqa, ps, dss, kpos, qpos, kv, acc, stage,
           r_sib, r_in, comb, ssem, rsem):
    me = lax.axis_index("ctx")
    core = lax.rem(me, 2)
    chip = me // 2
    x = lax.rem(chip, 2)
    z = chip // 2
    zp, zm, z2 = lax.rem(z + 1, 4), lax.rem(z + 3, 4), lax.rem(z + 2, 4)

    def at(zz, xx, cc):
        return (zz * 2 + xx) * 2 + cc

    sib = at(z, x, 1 - core)
    across = at(z, 1 - x, core)
    up = at(zp, x, core)
    down = at(zm, x, core)
    far = at(z2, x, core)

    def copy(n, src, dst, where):
        return pltpu.make_async_remote_copy(
            src_ref=src, dst_ref=dst, send_sem=ssem.at[n], recv_sem=rsem.at[n],
            device_id={"ctx": where}, device_id_type=pl.DeviceIdType.MESH)

    half = ROWS // 2
    a_lo, a_hi = pl.ds(ROWS, half), pl.ds(ROWS + half, half)
    copies = [
        (kv.at[S_O, LO], kv.at[S_O, HI], sib),
        (kv.at[S_O, LO], kv.at[S_XANDZ, LO], across),
        (kv.at[S_O, LO], kv.at[S_PM, HI], up),
        (kv.at[S_O, LO], kv.at[S_PM, LO], down),
        (kv.at[S_PM, pl.ds(ROWS, half)], kv.at[S_XANDZ, a_lo], up),
        (kv.at[S_PM, pl.ds(half, half)], kv.at[S_XANDZ, a_hi], down),
        (kv.at[S_XANDZ, LO], kv.at[S_XPM, HI], up),
        (kv.at[S_XANDZ, LO], kv.at[S_XPM, LO], down),
        (kv.at[S_PM], kv.at[S_PM_SIB], sib),
        (kv.at[S_XANDZ, LO], kv.at[S_XANDZ_SIB, LO], sib),
        (kv.at[S_XANDZ, HI], kv.at[S_XANDZ_SIB, HI], sib),
        (kv.at[S_XANDZ, HI], kv.at[S_XZ, LO], across),
        (kv.at[S_XPM], kv.at[S_XPM_SIB], sib),
        (kv.at[S_XZ, LO], kv.at[S_XZ, HI], sib),
        (stage.at[S_O, 1], r_sib.at[0, 0], sib),
        (stage.at[S_PM_SIB], r_sib.at[1], sib),
        (stage.at[S_XZ, 1], r_sib.at[2, 0], sib),
        (stage.at[S_XPM_SIB], r_sib.at[3], sib),
        (stage.at[S_XANDZ_SIB], r_sib.at[4], sib),
        (comb.at[0], r_in.at[0], up),
        (comb.at[1], r_in.at[1], down),
        (comb.at[2], r_in.at[2], across),
        (comb.at[3], r_in.at[3], up),
        (comb.at[4], r_in.at[4], down),
        (comb.at[5], r_in.at[5], across),
        (comb.at[6], r_in.at[6], far),
    ]

    def start(*ns):
        for n in ns:
            copy(n, *copies[n]).start()

    def arrived(*ns):
        for n in ns:
            copy(n, *copies[n]).wait_recv()

    kv[S_O, 0:ROWS, 0:HD] = k_in[...]
    kv[S_O, 0:ROWS, HD:] = v_in[...]

    barrier = pltpu.get_barrier_semaphore()
    for other in (sib, across, up, down, far):
        pl.semaphore_signal(barrier, inc=1, device_id={"ctx": other},
                            device_id_type=pl.DeviceIdType.MESH)
    pl.semaphore_wait(barrier, 5)
    start(0, 1, 2, 3)

    row_iota = lax.broadcasted_iota(jnp.int32, (8, STRETCH), 1)
    col_iota = lax.broadcasted_iota(jnp.int32, (STRETCH, HD), 0)
    other_core = 1 - core
    other_x = 1 - x
    blocks = {
        S_O: (at(z, x, core), at(z, x, other_core)),
        S_PM: (at(zp, x, core), at(zm, x, core)),
        S_PM_SIB: (at(zp, x, other_core), at(zm, x, other_core)),
        S_XPM: (at(zp, other_x, core), at(zm, other_x, core)),
        S_XPM_SIB: (at(zp, other_x, other_core), at(zm, other_x, other_core)),
        S_XZ: (at(z2, other_x, core), at(z2, other_x, other_core)),
        S_XANDZ: (at(z, other_x, core), at(z2, x, core)),
        S_XANDZ_SIB: (at(z, other_x, other_core), at(z2, x, other_core)),
    }
    for s, owners in blocks.items():
        for b, owner in enumerate(owners):
            for t in range(2):
                c0 = b * ROWS + t * STRETCH
                kpos[s, :, c0 : c0 + STRETCH] = row_iota + order[owner * 2 + t] * STRETCH
    for t in range(2):
        qpos[t] = col_iota + order[me * 2 + t] * STRETCH

    norm = norm_in[...] * LOG2E
    norm_cols = jnp.concatenate([norm, norm], axis=0).T
    for h in range(HEADS):
        rows = slice(h * ROWS, (h + 1) * ROWS)
        cols = slice(h * HD, (h + 1) * HD)
        q = q_in[:, cols]
        do = do_in[:, cols]
        qh[rows, :] = q
        doh[rows, :] = do
        qt[:, rows] = q.T
        dot_[:, rows] = do.T
        delta = jnp.sum(do.astype(F32) * o_in[:, cols].astype(F32), axis=1, keepdims=True)
        nb[rows, :] = jnp.broadcast_to(norm_cols[:, h : h + 1], (ROWS, HD))
        dl[rows, :] = jnp.broadcast_to(delta, (ROWS, HD))
    dqa[...] = jnp.zeros_like(dqa)
    arrived(0)

    def rows_against(i, j):
        rows = slice(j * SUB, (j + 1) * SUB)
        k = kv[i, :, 0:HD]
        v = kv[i, :, HD:]
        s = dot(qh[rows, :], k, 1, 1)
        dp = dot(doh[rows, :], v, 1, 1)
        seen = kpos[i, 0:1, :] <= qpos[j % 2, :, 0:1]
        p = jnp.exp2(jnp.where(seen, s * (SCALE * LOG2E) - nb[rows, 0:1], HIDDEN))
        ds = (p * (dp - dl[rows, 0:1])).astype(BF16)
        ps[rows, :] = p.astype(BF16)
        dss[rows, :] = ds
        dqa[rows, :] += dot(ds, k)

    def combine(n, slot, part, sib_part, *arrivals):
        total = acc[slot, part] + sib_part[...].astype(F32)
        for r in arrivals:
            total += r_in[r].astype(F32)
        comb[n] = total.astype(BF16)

    def body(i, _):
        @pl.when(i == S_PM)
        def _():
            arrived(2, 3)
            start(4, 5, 8)
            arrived(1)
            start(6, 7, 9)

        @pl.when(i == S_PM_SIB)
        def _():
            arrived(8)
            arrived(4, 5)
            start(11, 10)

        @pl.when(i == S_XPM)
        def _():
            arrived(6, 7)
            start(12)

        @pl.when(i == S_XZ)
        def _():
            arrived(13)

        @pl.when(i == S_XPM_SIB)
        def _():
            arrived(12)

        @pl.when(i == S_XANDZ_SIB)
        def _():
            arrived(9, 10)

        for j in range(4):
            rows_against(i, j)

        @pl.when(i == S_XPM)
        def _():
            arrived(11)
            start(13)
            arrived(15)
            combine(0, S_PM, 0, r_sib.at[1, 0])
            combine(1, S_PM, 1, r_sib.at[1, 1])
            start(19, 20)

        @pl.when(i == S_XPM_SIB)
        def _():
            arrived(16)
            combine(2, S_XZ, 0, r_sib.at[2, 0])
            start(21)

        @pl.when(i == S_XANDZ_SIB)
        def _():
            arrived(17)
            combine(3, S_XPM, 0, r_sib.at[3, 0])
            combine(4, S_XPM, 1, r_sib.at[3, 1])
            start(22, 23)

        for j in range(4, 8):
            rows_against(i, j)
        dk = dot(qt[...], dss[...])
        dv = dot(dot_[...], ps[...])
        for part in range(2):
            cols = slice(part * ROWS, (part + 1) * ROWS)
            acc[i, part, 0:HD] = dk[:, cols]
            acc[i, part, HD:] = dv[:, cols]
            stage[i, part, 0:HD] = dk[:, cols].astype(BF16)
            stage[i, part, HD:] = dv[:, cols].astype(BF16)

        @pl.when(i == S_O)
        def _():
            start(14)

        @pl.when(i == S_PM_SIB)
        def _():
            start(15)

        @pl.when(i == S_XZ)
        def _():
            start(16)

        @pl.when(i == S_XPM_SIB)
        def _():
            start(17)

        @pl.when(i == S_XANDZ_SIB)
        def _():
            start(18)

        return 0

    lax.fori_loop(0, SLOTS, body, 0)
    arrived(18, 21)
    combine(6, S_XANDZ, 1, r_sib.at[4, 1], 2)
    start(25)
    arrived(22, 23)
    combine(5, S_XANDZ, 0, r_sib.at[4, 0], 3, 4)
    start(24)
    for h in range(HEADS):
        dq_out[:, h * HD : (h + 1) * HD] = (dqa[h * ROWS : (h + 1) * ROWS, :] * SCALE).astype(BF16)
    arrived(14, 19, 20)
    acc[S_O, 0] += r_sib[0, 0].astype(F32) + r_in[0].astype(F32) + r_in[1].astype(F32)
    arrived(24, 25)
    total = acc[S_O, 0] + r_in[5].astype(F32) + r_in[6].astype(F32)
    dk_out[...] = (total[0:HD] * SCALE).astype(BF16).T
    dv_out[...] = total[HD:].astype(BF16).T
    for n in range(len(copies)):
        copy(n, *copies[n]).wait_send()


def shards(queries, keys, values, outputs, out_grads, log_norms, stretch_order):
    rows = HEADS * ROWS
    vmem = pl.BlockSpec(memory_space=pltpu.VMEM)
    return pl.pallas_call(
        kernel,
        out_shape=[
            jax.ShapeDtypeStruct((ROWS, HEADS * HD), BF16),
            jax.ShapeDtypeStruct((ROWS, HD), BF16),
            jax.ShapeDtypeStruct((ROWS, HD), BF16),
        ],
        in_specs=[pl.BlockSpec(memory_space=pltpu.SMEM)] + [vmem] * 6,
        out_specs=[vmem] * 3,
        scratch_shapes=[
            pltpu.VMEM((rows, HD), BF16),
            pltpu.VMEM((rows, HD), BF16),
            pltpu.VMEM((HD, rows), BF16),
            pltpu.VMEM((HD, rows), BF16),
            pltpu.VMEM((rows, HD), F32),
            pltpu.VMEM((rows, HD), F32),
            pltpu.VMEM((rows, HD), F32),
            pltpu.VMEM((rows, KEYS), BF16),
            pltpu.VMEM((rows, KEYS), BF16),
            pltpu.VMEM((SLOTS, 8, KEYS), jnp.int32),
            pltpu.VMEM((2, STRETCH, HD), jnp.int32),
            pltpu.VMEM((SLOTS, KEYS, 2 * HD), BF16),
            pltpu.VMEM((SLOTS, 2, 2 * HD, ROWS), F32),
            pltpu.VMEM((SLOTS, 2, 2 * HD, ROWS), BF16),
            pltpu.VMEM((5, 2, 2 * HD, ROWS), BF16),
            pltpu.VMEM((7, 2 * HD, ROWS), BF16),
            pltpu.VMEM((7, 2 * HD, ROWS), BF16),
            pltpu.SemaphoreType.DMA((26,)),
            pltpu.SemaphoreType.DMA((26,)),
        ],
        compiler_params=pltpu.CompilerParams(
            vmem_limit_bytes=58 * 2**20, collective_id=0, has_side_effects=True
        ),
    )(stretch_order, queries, out_grads, outputs, log_norms, keys, values)


def solution(mesh):
    return jax.shard_map(
        shards,
        mesh=mesh,
        in_specs=(
            P(("dp", "ctx"), "tp"),
            P(("dp", "ctx"), "tp"),
            P(("dp", "ctx"), "tp"),
            P(("dp", "ctx"), "tp"),
            P(("dp", "ctx"), "tp"),
            P("tp", ("dp", "ctx")),
            P("dp"),
        ),
        out_specs=(P(("dp", "ctx"), "tp"), P(("dp", "ctx"), "tp"), P(("dp", "ctx"), "tp")),
        check_vma=False,
    )
```

time: 210 us -> 66.2 us (0.32)
  waiting for transfers between devices: 144 us -> 0 us
  Pallas kernels: 47.7 us -> 61.9 us
  between operations: 13.8 us -> 0.65 us
    all_gather x2 -> x0, waiting for transfers between devices: 72.6 us -> none  [the longest x1 36.9 us: shards(): key_all = lax.all_gather(keys, 'ctx', axis=0, tiled=True)]
    reduce_scatter x1 -> x0, waiting for transfers between devices: 70.2 us -> none  [shards(): summed = lax.psum_scatter(term, 'ctx', scatter_dimension=0, tiled=True)]
    pallas_call x1, Pallas kernels: 47.7 us -> 61.9 us  [shards(): pl.pallas_call(kernel, out_shape=[jax.ShapeDtypeStruct((ROWS, HEADS * HD)...]
    unnamed x1 -> x7, local copies, waits for them, and re-layouts: 0.02 us -> 3.51 us
  transfers between devices with their start and end apart: 3 -> 0, of which waited for: 3 -> 0; matrix products, arithmetic and copies ran while one was open for 0% -> 0% of each run, Pallas kernels for 0% -> 0%
where the time goes in v2:
time: 66.2 us; the launch traced here: 66.1 us
  Pallas kernels  61.9 us (94%)
  local copies, waits for them, and re-layouts  3.51 us (5%)
    pallas_call x1, Pallas kernels, shards(): pl.pallas_call(kernel, out_shape=[jax.ShapeDtypeStruct((ROWS, HEADS * HD)...  61.9 us
    unnamed x7, local copies, waits for them, and re-layouts  3.51 us

profile of v2, /device:TPU:0, one launch (start us, length us, event | category | flops | bytes accessed | tf_op | source)
XLA Modules:
  0.0 66.1 jit_solution(1310656545310549935)
XLA Ops:
  0.6 61.9 %shard_map.94 = (bf16[512,512]{1,0:T(8,128)(2,1)}, bf16[512,128]{1,0:T(8,128)(2,1)}, bf16[512,128]{1,0:T(8,128)(2,1)}) custom-call(s32[32]{0:T(128)} %order.1, bf16[512,512]{1,0:T(8,128)(2,1)} %q_in.1, bf16[512,512]{1,0:T(8,128)(2,1)} %do_in.1, bf16[512,512]{1,0:T(8,128)(2,1)} %o_in.1, f32[4,512]{1,0:T(4,128)} %norm_in.1, bf16[512,128]{1,0:T(8,128)(2,1)} %k_in.1, ...), custom_call_target="tpu_custom_call" | custom-call | tf_op jit(solution)/shard_map/pallas_call | solution.py:272
  62.5 0.0 copy-start.1
  62.6 1.9 %copy.13 = bf16[512,512]{1,0:T(8,128)(2,1)} copy(bf16[512,512]{1,0:T(8,128)(2,1)} %get-tuple-element.6) | data formatting | bytes 1048576
  64.5 0.0 copy-done.1
  64.5 0.0 copy-start
  64.5 0.7 copy.14
  65.1 0.3 copy-done
  65.4 0.7 copy.15
Async XLA Ops:
  62.5 1.9 %copy-start.1 = (bf16[512,128]{1,0:T(8,128)(2,1)S(1)}, bf16[512,128]{1,0:T(8,128)(2,1)}, u32[]{:S(2)}) copy-start(bf16[512,128]{1,0:T(8,128)(2,1)} %get-tuple-element.7) | copy-start | bytes 393220
  64.5 1.0 %copy-start = (bf16[512,128]{1,0:T(8,128)(2,1)S(1)}, bf16[512,128]{1,0:T(8,128)(2,1)}, u32[]{:S(2)}) copy-start(bf16[512,128]{1,0:T(8,128)(2,1)} %get-tuple-element.8) | copy-start | bytes 393220

commit v3 on v2

--- a/solution.py
+++ b/solution.py
@@ -12,6 +12,7 @@
 KEYS = 1024
 SUB = 256
 SLOTS = 8
+HALF = 1024
 F32 = jnp.float32
 BF16 = jnp.bfloat16
 LOG2E = 1.4426950408889634
@@ -28,8 +29,8 @@
 
 
 def kernel(order, q_in, do_in, o_in, norm_in, k_in, v_in, dq_out, dk_out, dv_out,
-           qh, doh, qt, dot_, nb, dl, dqa, ps, dss, kpos, qpos, kv, acc, stage,
-           r_sib, r_in, comb, ssem, rsem):
+           qh, doh, oh, qt, dot_, nb, dl, dqa, ps, dss, kpos, qpos, kv, acc, stage,
+           r_sib, r_in, comb, dqb, dkb, dvb, ssem, rsem, isem, osem):
     me = lax.axis_index("ctx")
     core = lax.rem(me, 2)
     chip = me // 2
@@ -90,15 +91,24 @@
         for n in ns:
             copy(n, *copies[n]).wait_recv()
 
-    kv[S_O, 0:ROWS, 0:HD] = k_in[...]
-    kv[S_O, 0:ROWS, HD:] = v_in[...]
-
     barrier = pltpu.get_barrier_semaphore()
     for other in (sib, across, up, down, far):
         pl.semaphore_signal(barrier, inc=1, device_id={"ctx": other},
                             device_id_type=pl.DeviceIdType.MESH)
+    loads = [(k_in, kv.at[S_O, LO, pl.ds(0, HD)]), (v_in, kv.at[S_O, LO, pl.ds(HD, HD)])]
+    for h in range(HEADS):
+        cols, rows = pl.ds(h * HD, HD), pl.ds(h * ROWS, ROWS)
+        loads += [(q_in.at[:, cols], qh.at[rows]), (do_in.at[:, cols], doh.at[rows]),
+                  (o_in.at[:, cols], oh.at[rows])]
+    loads = [pltpu.make_async_copy(src, dst, isem.at[n]) for n, (src, dst) in enumerate(loads)]
+    for load in loads:
+        load.start()
+    loads[0].wait()
+    loads[1].wait()
     pl.semaphore_wait(barrier, 5)
     start(0, 1, 2, 3)
+    acc[...] = jnp.zeros_like(acc)
+    dqa[...] = jnp.zeros_like(dqa)
 
     row_iota = lax.broadcasted_iota(jnp.int32, (8, STRETCH), 1)
     col_iota = lax.broadcasted_iota(jnp.int32, (STRETCH, HD), 0)
@@ -124,33 +134,46 @@
 
     norm = norm_in[...] * LOG2E
     norm_cols = jnp.concatenate([norm, norm], axis=0).T
+    for load in loads[2:]:
+        load.wait()
     for h in range(HEADS):
         rows = slice(h * ROWS, (h + 1) * ROWS)
-        cols = slice(h * HD, (h + 1) * HD)
-        q = q_in[:, cols]
-        do = do_in[:, cols]
-        qh[rows, :] = q
-        doh[rows, :] = do
-        qt[:, rows] = q.T
+        do = doh[rows, :]
+        qt[:, rows] = qh[rows, :].T
         dot_[:, rows] = do.T
-        delta = jnp.sum(do.astype(F32) * o_in[:, cols].astype(F32), axis=1, keepdims=True)
+        delta = jnp.sum(do.astype(F32) * oh[rows, :].astype(F32), axis=1, keepdims=True)
         nb[rows, :] = jnp.broadcast_to(norm_cols[:, h : h + 1], (ROWS, HD))
         dl[rows, :] = jnp.broadcast_to(delta, (ROWS, HD))
-    dqa[...] = jnp.zeros_like(dqa)
     arrived(0)
 
-    def rows_against(i, j):
-        rows = slice(j * SUB, (j + 1) * SUB)
-        k = kv[i, :, 0:HD]
-        v = kv[i, :, HD:]
-        s = dot(qh[rows, :], k, 1, 1)
-        dp = dot(doh[rows, :], v, 1, 1)
-        seen = kpos[i, 0:1, :] <= qpos[j % 2, :, 0:1]
-        p = jnp.exp2(jnp.where(seen, s * (SCALE * LOG2E) - nb[rows, 0:1], HIDDEN))
-        ds = (p * (dp - dl[rows, 0:1])).astype(BF16)
-        ps[rows, :] = p.astype(BF16)
-        dss[rows, :] = ds
-        dqa[rows, :] += dot(ds, k)
+    def wide(a):
+        return jnp.concatenate([a] * (KEYS // HD), axis=1)
+
+    def compute(slot, row0):
+        for j in range(HALF // SUB):
+            rows = pl.ds(pl.multiple_of(row0 + j * SUB, SUB), SUB)
+            part_rows = slice(j * SUB, (j + 1) * SUB)
+            k = kv[slot, :, 0:HD]
+            v = kv[slot, :, HD:]
+            s = dot(qh[rows, :], k, 1, 1)
+            dp = dot(doh[rows, :], v, 1, 1)
+            seen = kpos[slot, 0:1, :] <= wide(qpos[j % 2])
+            p = jnp.exp2(jnp.where(seen, s * (SCALE * LOG2E) - wide(nb[rows, :]), HIDDEN))
+            ds = (p * (dp - wide(dl[rows, :]))).astype(BF16)
+            ps[part_rows, :] = p.astype(BF16)
+            dss[part_rows, :] = ds
+            dqa[rows, :] += dot(ds, k)
+        rows = pl.ds(pl.multiple_of(row0, HALF), HALF)
+        dk = dot(qt[:, rows], dss[...])
+        dv = dot(dot_[:, rows], ps[...])
+        for part in range(2):
+            cols = slice(part * ROWS, (part + 1) * ROWS)
+            dk_sum = acc[slot, part, 0:HD] + dk[:, cols]
+            dv_sum = acc[slot, part, HD:] + dv[:, cols]
+            acc[slot, part, 0:HD] = dk_sum
+            acc[slot, part, HD:] = dv_sum
+            stage[slot, part, 0:HD] = dk_sum.astype(BF16)
+            stage[slot, part, HD:] = dv_sum.astype(BF16)
 
     def combine(n, slot, part, sib_part, *arrivals):
         total = acc[slot, part] + sib_part[...].astype(F32)
@@ -158,41 +181,27 @@
             total += r_in[r].astype(F32)
         comb[n] = total.astype(BF16)
 
-    def body(i, _):
-        @pl.when(i == S_PM)
+    def body(t, _):
+        @pl.when(t == 1)
         def _():
             arrived(2, 3)
             start(4, 5, 8)
             arrived(1)
             start(6, 7, 9)
 
-        @pl.when(i == S_PM_SIB)
+        @pl.when(t == 3)
         def _():
             arrived(8)
             arrived(4, 5)
             start(11, 10)
 
-        @pl.when(i == S_XPM)
-        def _():
+        @pl.when(t == 5)
+        def _():
+            start(15)
             arrived(6, 7)
             start(12)
 
-        @pl.when(i == S_XZ)
-        def _():
-            arrived(13)
-
-        @pl.when(i == S_XPM_SIB)
-        def _():
-            arrived(12)
-
-        @pl.when(i == S_XANDZ_SIB)
-        def _():
-            arrived(9, 10)
-
-        for j in range(4):
-            rows_against(i, j)
-
-        @pl.when(i == S_XPM)
+        @pl.when(t == 6)
         def _():
             arrived(11)
             start(13)
@@ -201,84 +210,95 @@
             combine(1, S_PM, 1, r_sib.at[1, 1])
             start(19, 20)
 
-        @pl.when(i == S_XPM_SIB)
+        @pl.when(t == 7)
+        def _():
+            arrived(13)
+
+        @pl.when(t == 9)
+        def _():
+            start(16)
+            arrived(12)
+
+        @pl.when(t == 10)
         def _():
             arrived(16)
             combine(2, S_XZ, 0, r_sib.at[2, 0])
             start(21)
 
-        @pl.when(i == S_XANDZ_SIB)
+        @pl.when(t == 11)
+        def _():
+            start(17)
+            arrived(9, 10)
+
+        @pl.when(t == 12)
         def _():
             arrived(17)
             combine(3, S_XPM, 0, r_sib.at[3, 0])
             combine(4, S_XPM, 1, r_sib.at[3, 1])
             start(22, 23)
 
-        for j in range(4, 8):
-            rows_against(i, j)
-        dk = dot(qt[...], dss[...])
-        dv = dot(dot_[...], ps[...])
-        for part in range(2):
-            cols = slice(part * ROWS, (part + 1) * ROWS)
-            acc[i, part, 0:HD] = dk[:, cols]
-            acc[i, part, HD:] = dv[:, cols]
-            stage[i, part, 0:HD] = dk[:, cols].astype(BF16)
-            stage[i, part, HD:] = dv[:, cols].astype(BF16)
-
-        @pl.when(i == S_O)
-        def _():
-            start(14)
-
-        @pl.when(i == S_PM_SIB)
-        def _():
-            start(15)
-
-        @pl.when(i == S_XZ)
-        def _():
-            start(16)
-
-        @pl.when(i == S_XPM_SIB)
-        def _():
-            start(17)
-
-        @pl.when(i == S_XANDZ_SIB)
+        @pl.when(t == 13)
         def _():
             start(18)
 
+        @pl.when(t == 15)
+        def _():
+            arrived(18, 21)
+            combine(6, S_XANDZ, 1, r_sib.at[4, 1], 2)
+            start(25)
+            arrived(22, 23)
+            combine(5, S_XANDZ, 0, r_sib.at[4, 0], 3, 4)
+            start(24)
+
+        compute(lax.rem((t + 1) // 2, SLOTS), lax.rem(t + 1, 2) * HALF)
         return 0
 
-    lax.fori_loop(0, SLOTS, body, 0)
-    arrived(18, 21)
-    combine(6, S_XANDZ, 1, r_sib.at[4, 1], 2)
-    start(25)
-    arrived(22, 23)
-    combine(5, S_XANDZ, 0, r_sib.at[4, 0], 3, 4)
-    start(24)
+    lax.fori_loop(0, 2 * SLOTS, body, 0)
+    start(14)
+    outs = []
     for h in range(HEADS):
-        dq_out[:, h * HD : (h + 1) * HD] = (dqa[h * ROWS : (h + 1) * ROWS, :] * SCALE).astype(BF16)
-    arrived(14, 19, 20)
+        cols = slice(h * HD, (h + 1) * HD)
+        dqb[:, cols] = (dqa[h * ROWS : (h + 1) * ROWS, :] * SCALE).astype(BF16)
+    outs.append(pltpu.make_async_copy(dqb, dq_out, osem.at[0]))
+    outs[0].start()
+    arrived(19, 20, 14)
     acc[S_O, 0] += r_sib[0, 0].astype(F32) + r_in[0].astype(F32) + r_in[1].astype(F32)
     arrived(24, 25)
     total = acc[S_O, 0] + r_in[5].astype(F32) + r_in[6].astype(F32)
-    dk_out[...] = (total[0:HD] * SCALE).astype(BF16).T
-    dv_out[...] = total[HD:].astype(BF16).T
+    dkb[...] = (total[0:HD] * SCALE).astype(BF16).T
+    dvb[...] = total[HD:].astype(BF16).T
+    outs.append(pltpu.make_async_copy(dkb, dk_out, osem.at[1]))
+    outs.append(pltpu.make_async_copy(dvb, dv_out, osem.at[2]))
+    outs[1].start()
+    outs[2].start()
     for n in range(len(copies)):
         copy(n, *copies[n]).wait_send()
+    for out in outs:
+        out.wait()
+
+
+def hand_over(dq, dk, dv, dq_out, dk_out, dv_out):
+    dq_out[...] = dq[...]
+    dk_out[...] = dk[...]
+    dv_out[...] = dv[...]
 
 
 def shards(queries, keys, values, outputs, out_grads, log_norms, stretch_order):
     rows = HEADS * ROWS
-    vmem = pl.BlockSpec(memory_space=pltpu.VMEM)
-    return pl.pallas_call(
+    anywhere = pl.BlockSpec(memory_space=pl.ANY)
+    shapes = [
+        jax.ShapeDtypeStruct((ROWS, HEADS * HD), BF16),
+        jax.ShapeDtypeStruct((ROWS, HD), BF16),
+        jax.ShapeDtypeStruct((ROWS, HD), BF16),
+    ]
+    grads = pl.pallas_call(
         kernel,
-        out_shape=[
-            jax.ShapeDtypeStruct((ROWS, HEADS * HD), BF16),
-            jax.ShapeDtypeStruct((ROWS, HD), BF16),
-            jax.ShapeDtypeStruct((ROWS, HD), BF16),
-        ],
-        in_specs=[pl.BlockSpec(memory_space=pltpu.SMEM)] + [vmem] * 6,
-        out_specs=[vmem] * 3,
+        out_shape=shapes,
+        in_specs=[pl.BlockSpec(memory_space=pltpu.SMEM), anywhere, anywhere, anywhere,
+                  pl.BlockSpec(memory_space=pltpu.VMEM), anywhere, anywhere],
+        out_specs=[anywhere] * 3,
         scratch_shapes=[
+            pltpu.VMEM((rows, HD), BF16),
             pltpu.VMEM((rows, HD), BF16),
             pltpu.VMEM((rows, HD), BF16),
             pltpu.VMEM((HD, rows), BF16),
@@ -286,8 +306,8 @@
             pltpu.VMEM((rows, HD), F32),
             pltpu.VMEM((rows, HD), F32),
             pltpu.VMEM((rows, HD), F32),
-            pltpu.VMEM((rows, KEYS), BF16),
-            pltpu.VMEM((rows, KEYS), BF16),
+            pltpu.VMEM((HALF, KEYS), BF16),
+            pltpu.VMEM((HALF, KEYS), BF16),
             pltpu.VMEM((SLOTS, 8, KEYS), jnp.int32),
             pltpu.VMEM((2, STRETCH, HD), jnp.int32),
             pltpu.VMEM((SLOTS, KEYS, 2 * HD), BF16),
@@ -296,13 +316,24 @@
             pltpu.VMEM((5, 2, 2 * HD, ROWS), BF16),
             pltpu.VMEM((7, 2 * HD, ROWS), BF16),
             pltpu.VMEM((7, 2 * HD, ROWS), BF16),
+            pltpu.VMEM((ROWS, HEADS * HD), BF16),
+            pltpu.VMEM((ROWS, HD), BF16),
+            pltpu.VMEM((ROWS, HD), BF16),
             pltpu.SemaphoreType.DMA((26,)),
             pltpu.SemaphoreType.DMA((26,)),
+            pltpu.SemaphoreType.DMA((14,)),
+            pltpu.SemaphoreType.DMA((3,)),
         ],
         compiler_params=pltpu.CompilerParams(
             vmem_limit_bytes=58 * 2**20, collective_id=0, has_side_effects=True
         ),
     )(stretch_order, queries, out_grads, outputs, log_norms, keys, values)
+    return pl.pallas_call(
+        hand_over,
+        out_shape=shapes,
+        in_specs=[pl.BlockSpec(memory_space=pltpu.VMEM)] * 3,
+        out_specs=[pl.BlockSpec(memory_space=pltpu.VMEM)] * 3,
+    )(*grads)
 
 
 def solution(mesh):

time: 66.2 us -> 62.1 us (0.938)
  local copies, waits for them, and re-layouts: 3.51 us -> 0 us
    unnamed x7 -> x0, local copies, waits for them, and re-layouts: 3.51 us -> none
    pallas_call x1 -> x2, Pallas kernels: 61.9 us -> 61.3 us  [the longest x1 59.3 us: shards(): pl.pallas_call(kernel, out_shape=shapes, in_specs=[pl.BlockSpec(memory_sp...]
where the time goes in v3:
time: 62.1 us; the launch traced here: 61.9 us
  Pallas kernels  61.3 us (99%)
  between operations  0.64 us (1%)
    pallas_call x1, Pallas kernels, shards(): pl.pallas_call(kernel, out_shape=shapes, in_specs=[pl.BlockSpec(memory_sp...  59.3 us
    pallas_call x1, Pallas kernels, shards(): pl.pallas_call(hand_over, out_shape=shapes, in_specs=[pl.BlockSpec(memory...  2.01 us

profile of v3, /device:TPU:0, one launch (start us, length us, event | category | flops | bytes accessed | tf_op | source)
XLA Modules:
  0.0 61.9 jit_solution(15880256419480520782)
XLA Ops:
  0.6 59.3 %shard_map.94 = (bf16[512,512]{1,0:T(8,128)(2,1)}, bf16[512,128]{1,0:T(8,128)(2,1)}, bf16[512,128]{1,0:T(8,128)(2,1)}) custom-call(s32[32]{0:T(128)} %order.1, bf16[512,512]{1,0:T(8,128)(2,1)} %q_in.1, bf16[512,512]{1,0:T(8,128)(2,1)} %do_in.1, bf16[512,512]{1,0:T(8,128)(2,1)} %o_in.1, f32[4,512]{1,0:T(4,128)} %norm_in.1, bf16[512,128]{1,0:T(8,128)(2,1)} %k_in.1, ...), custom_call_target="tpu_custom_call" | custom-call | tf_op jit(solution)/shard_map/pallas_call | solution.py:294
  59.9 2.0 %shard_map.95 = (bf16[512,512]{1,0:T(8,128)(2,1)}, bf16[512,128]{1,0:T(8,128)(2,1)}, bf16[512,128]{1,0:T(8,128)(2,1)}) custom-call(bf16[512,512]{1,0:T(8,128)(2,1)} %get-tuple-element.6.dq, bf16[512,128]{1,0:T(8,128)(2,1)} %get-tuple-element.7.dk, bf16[512,128]{1,0:T(8,128)(2,1)} %get-tuple-element.8.dv), custom_call_target="tpu_custom_call" | custom-call | tf_op jit(solution)/shard_map/pallas_call | solution.py:331

commit v4 on v1

v4 whole, which is shorter than its diff:
```python
import jax
import jax.numpy as jnp
from jax import lax
from jax.experimental import pallas as pl
from jax.experimental.pallas import tpu as pltpu
from jax.sharding import PartitionSpec

HD = 128
HEADS = 4
STRETCH = 256
ROWS = 512
KEYS = 512
STEPS = 16
F32 = jnp.float32
BF16 = jnp.bfloat16
LOG2E = 1.4426950408889634
SCALE = HD ** (-0.5)
HIDDEN = -1e30
FIRST = pl.ds(0, STRETCH)
SECOND = pl.ds(STRETCH, STRETCH)
HALVES = (FIRST, SECOND)

O, P0, P1, P0S, P1S, R0, R1, R0S, XZ, XZS, R1S, Q0S, Q1S, Q0, Q1, OS = range(STEPS)
P, PS, R, RS, Q, QS = (P0, P1), (P0S, P1S), (R0, R1), (R0S, R1S), (Q0, Q1), (Q0S, Q1S)


def dot(a, b, ca=1, cb=0):
    return lax.dot_general(a, b, (((ca,), (cb,)), ((), ())), preferred_element_type=F32)


def kernel(order, q_in, do_in, o_in, norm_in, k_in, v_in, dq_out, dk_out, dv_out,
           qh, doh, oh, qt, dot_, nb, dl, dqa, ps, dss, kpos, qpos, kv, acc, stage,
           r_sib, r_in, comb, r_xz, comb_xz, dqb, dkb, dvb, ssem, rsem, isem, osem):
    me = lax.axis_index("ctx")
    core = lax.rem(me, 2)
    chip = me // 2
    x = lax.rem(chip, 2)
    z = chip // 2
    zp, zm, z2 = lax.rem(z + 1, 4), lax.rem(z + 3, 4), lax.rem(z + 2, 4)

    def at(zz, xx, cc):
        return (zz * 2 + xx) * 2 + cc

    sib = at(z, x, 1 - core)
    across = at(z, 1 - x, core)
    up = at(zp, x, core)
    down = at(zm, x, core)
    far = at(z2, x, core)

    def copy(n, src, dst, where):
        return pltpu.make_async_remote_copy(
            src_ref=src, dst_ref=dst, send_sem=ssem.at[n], recv_sem=rsem.at[n],
            device_id={"ctx": where}, device_id_type=pl.DeviceIdType.MESH)

    copies = {"o": (kv.at[O], kv.at[OS], sib), "xz": (kv.at[XZ], kv.at[XZS], sib),
              "x2": (comb_xz, r_xz, across), "os": (stage.at[OS], r_sib.at[0], sib),
              "xzs": (stage.at[XZS], r_sib.at[5], sib),
              "z0": (kv.at[P0, SECOND], kv.at[Q0, SECOND], up),
              "z1": (kv.at[P1, FIRST], kv.at[Q1, SECOND], down)}
    for h in range(2):
        own = kv.at[O, HALVES[h]]
        copies |= {
            f"ou{h}": (own, kv.at[P[h], SECOND], up),
            f"od{h}": (own, kv.at[P[h], FIRST], down),
            f"ox{h}": (own, kv.at[Q[h], FIRST], across),
            f"xu{h}": (kv.at[Q[h], FIRST], kv.at[R[h], SECOND], up),
            f"xd{h}": (kv.at[Q[h], FIRST], kv.at[R[h], FIRST], down),
            f"zx{h}": (kv.at[Q[h], SECOND], kv.at[XZ, HALVES[h]], across),
            f"p{h}": (kv.at[P[h]], kv.at[PS[h]], sib),
            f"q{h}": (kv.at[Q[h]], kv.at[QS[h]], sib),
            f"r{h}": (kv.at[R[h]], kv.at[RS[h]], sib),
            f"ps{h}": (stage.at[PS[h]], r_sib.at[1 + h], sib),
            f"rs{h}": (stage.at[RS[h]], r_sib.at[3 + h], sib),
            f"qs{h}": (stage.at[QS[h]], r_sib.at[6 + h], sib),
            f"pu{h}": (comb.at[h, 0], r_in.at[h, 0], up),
            f"pd{h}": (comb.at[h, 1], r_in.at[h, 1], down),
            f"ru{h}": (comb.at[2 + h, 0], r_in.at[2 + h, 0], up),
            f"rd{h}": (comb.at[2 + h, 1], r_in.at[2 + h, 1], down),
            f"qx{h}": (comb.at[4 + h, 0], r_in.at[4 + h, 0], across),
            f"qz{h}": (comb.at[4 + h, 1], r_in.at[4 + h, 1], far),
        }
    number = {name: n for n, name in enumerate(copies)}

    def start(names):
        for name in names.split():
            copy(number[name], *copies[name]).start()

    def arrived(names):
        for name in names.split():
            copy(number[name], *copies[name]).wait_recv()

    barrier = pltpu.get_barrier_semaphore()
    for other in (sib, across, up, down, far):
        pl.semaphore_signal(barrier, inc=1, device_id={"ctx": other},
                            device_id_type=pl.DeviceIdType.MESH)
    loads = [(k_in, kv.at[O, :, pl.ds(0, HD)]), (v_in, kv.at[O, :, pl.ds(HD, HD)])]
    for h in range(HEADS):
        cols, rows = pl.ds(h * HD, HD), pl.ds(h * ROWS, ROWS)
        loads += [(q_in.at[:, cols], qh.at[rows]), (do_in.at[:, cols], doh.at[rows]),
                  (o_in.at[:, cols], oh.at[rows])]
    loads = [pltpu.make_async_copy(src, dst, isem.at[n]) for n, (src, dst) in enumerate(loads)]
    for load in loads:
        load.start()
    loads[0].wait()
    loads[1].wait()
    pl.semaphore_wait(barrier, 5)
    start("ou0 od0 ox0 ou1 od1 ox1 o")
    dqa[...] = jnp.zeros_like(dqa)

    row_iota = lax.broadcasted_iota(jnp.int32, (8, STRETCH), 1)
    col_iota = lax.broadcasted_iota(jnp.int32, (STRETCH, HD), 0)
    other_core = 1 - core
    other_x = 1 - x
    blocks = {O: (me * 2, me * 2 + 1), OS: (sib * 2, sib * 2 + 1)}
    blocks[XZ] = tuple(at(z2, other_x, core) * 2 + h for h in range(2))
    blocks[XZS] = tuple(at(z2, other_x, other_core) * 2 + h for h in range(2))
    for h in range(2):
        for block, c in ((P[h], core), (PS[h], other_core)):
            blocks[block] = (at(zp, x, c) * 2 + h, at(zm, x, c) * 2 + h)
        for block, c in ((R[h], core), (RS[h], other_core)):
            blocks[block] = (at(zp, other_x, c) * 2 + h, at(zm, other_x, c) * 2 + h)
        for block, c in ((Q[h], core), (QS[h], other_core)):
            blocks[block] = (at(z, other_x, c) * 2 + h, at(z2, x, c) * 2 + h)
    for block, stretches in blocks.items():
        for h, stretch in enumerate(stretches):
            cols = slice(h * STRETCH, (h + 1) * STRETCH)
            kpos[block, :, cols] = row_iota + order[stretch] * STRETCH
    for h in range(2):
        qpos[h * STRETCH : (h + 1) * STRETCH] = col_iota + order[me * 2 + h] * STRETCH

    norm = norm_in[...] * LOG2E
    norm_cols = jnp.concatenate([norm, norm], axis=0).T
    for load in loads[2:]:
        load.wait()
    for h in range(HEADS):
        rows = slice(h * ROWS, (h + 1) * ROWS)
        do = doh[rows, :]
        qt[:, rows] = qh[rows, :].T
        dot_[:, rows] = do.T
        delta = jnp.sum(do.astype(F32) * oh[rows, :].astype(F32), axis=1, keepdims=True)
        nb[rows, :] = jnp.broadcast_to(norm_cols[:, h : h + 1], (ROWS, HD))
        dl[rows, :] = jnp.broadcast_to(delta, (ROWS, HD))

    def wide(a):
        return jnp.concatenate([a] * (KEYS // HD), axis=1)

    def compute(b):
        for h in range(HEADS):
            rows = slice(h * ROWS, (h + 1) * ROWS)
            k = kv[b, :, 0:HD]
            v = kv[b, :, HD:]
            s = dot(qh[rows, :], k, 1, 1)
            dp = dot(doh[rows, :], v, 1, 1)
            seen = kpos[b, 0:1, :] <= wide(qpos[...])
            p = jnp.exp2(jnp.where(seen, s * (SCALE * LOG2E) - wide(nb[rows, :]), HIDDEN))
            ds = (p * (dp - wide(dl[rows, :]))).astype(BF16)
            ps[rows, :] = p.astype(BF16)
            dss[rows, :] = ds
            dqa[rows, :] += dot(ds, k)
        dk = dot(qt[...], dss[...])
        dv = dot(dot_[...], ps[...])
        acc[b, 0:HD] = dk
        acc[b, HD:] = dv
        stage[b, 0:HD] = dk.astype(BF16)
        stage[b, HD:] = dv.astype(BF16)

    def combine(n, block, sib_part):
        total = acc[block] + r_sib[sib_part].astype(F32)
        for part in range(2):
            cols = slice(part * STRETCH, (part + 1) * STRETCH)
            comb[n, part] = total[:, cols].astype(BF16)

    def combine_q(h):
        cols = slice(h * STRETCH, (h + 1) * STRETCH)
        total = acc[Q[h]] + r_sib[6 + h].astype(F32)
        comb[4 + h, 0] = (total[:, :STRETCH] + r_in[2 + h, 0].astype(F32)
                          + r_in[2 + h, 1].astype(F32)).astype(BF16)
        comb[4 + h, 1] = (total[:, STRETCH:] + r_xz[:, cols].astype(F32)).astype(BF16)

    def before(t):
        if t == P0:
            arrived("ou0 od0")
            start("z0 p0")
            arrived("ox0")
            start("xd0")
        if t == P1:
            arrived("ou1 od1")
            start("z1 xu0 p1")
        if t == P0S:
            arrived("ox1")
            start("xu1 xd1")
            arrived("p0")
        if t == P1S:
            start("ps0")
            arrived("p1 z0 z1")
            start("zx0 zx1 q0 q1")
        if t == R0:
            start("ps1")
            arrived("xu0 xd0")
            start("r0")
            arrived("ps0")
            combine(0, P0, 1)
            start("pu0 pd0")
        if t == R1:
            arrived("xu1 xd1")
            start("r1")
            arrived("ps1")
            combine(1, P1, 2)
            start("pu1 pd1")
        if t == R0S:
            arrived("r0")
        if t == XZ:
            start("rs0")
            arrived("zx0 zx1")
            start("xz")
        if t == XZS:
            arrived("xz rs0")
            combine(2, R0, 3)
            start("ru0 rd0")
        if t == R1S:
            start("xzs")
            arrived("r1")
        if t == Q0S:
            start("rs1")
            arrived("xzs")
            comb_xz[...] = (acc[XZ] + r_sib[5].astype(F32)).astype(BF16)
            start("x2")
            arrived("q0")
        if t == Q1S:
            start("qs0")
            arrived("rs1")
            combine(3, R1, 4)
            start("ru1 rd1")
            arrived("q1")
        if t == Q0:
            start("qs1")
        if t == Q1:
            arrived("qs0 ru0 rd0 x2")
            combine_q(0)
            start("qx0 qz0")
        if t == OS:
            arrived("qs1 ru1 rd1")
            combine_q(1)
            start("qx1 qz1")
            arrived("o")

    def body(t, _):
        for n in range(1, STEPS):
            pl.when(t == n)(lambda n=n: before(n))
        compute(t)
        return 0

    lax.fori_loop(0, STEPS, body, 0)
    start("os")
    outs = []
    for h in range(HEADS):
        cols = slice(h * HD, (h + 1) * HD)
        dqb[:, cols] = (dqa[h * ROWS : (h + 1) * ROWS, :] * SCALE).astype(BF16)
    outs.append(pltpu.make_async_copy(dqb, dq_out, osem.at[0]))
    outs[0].start()
    arrived("os pu0 pd0 pu1 pd1")
    for h in range(2):
        cols = slice(h * STRETCH, (h + 1) * STRETCH)
        acc[O, :, cols] += (r_sib[0, :, cols].astype(F32) + r_in[h, 0].astype(F32)
                            + r_in[h, 1].astype(F32))
    arrived("qx0 qz0")
    acc[O, :, 0:STRETCH] += r_in[4, 0].astype(F32) + r_in[4, 1].astype(F32)
    arrived("qx1 qz1")
    acc[O, :, STRETCH:] += r_in[5, 0].astype(F32) + r_in[5, 1].astype(F32)
    total = acc[O]
    dkb[...] = (total[0:HD] * SCALE).astype(BF16).T
    dvb[...] = total[HD:].astype(BF16).T
    outs.append(pltpu.make_async_copy(dkb, dk_out, osem.at[1]))
    outs.append(pltpu.make_async_copy(dvb, dv_out, osem.at[2]))
    outs[1].start()
    outs[2].start()
    for name in copies:
        copy(number[name], *copies[name]).wait_send()
    for out in outs:
        out.wait()


def hand_over(dq, dk, dv, dq_out, dk_out, dv_out):
    dq_out[...] = dq[...]
    dk_out[...] = dk[...]
    dv_out[...] = dv[...]


def shards(queries, keys, values, outputs, out_grads, log_norms, stretch_order):
    rows = HEADS * ROWS
    anywhere = pl.BlockSpec(memory_space=pl.ANY)
    shapes = [
        jax.ShapeDtypeStruct((ROWS, HEADS * HD), BF16),
        jax.ShapeDtypeStruct((ROWS, HD), BF16),
        jax.ShapeDtypeStruct((ROWS, HD), BF16),
    ]
    grads = pl.pallas_call(
        kernel,
        out_shape=shapes,
        in_specs=[pl.BlockSpec(memory_space=pltpu.SMEM), anywhere, anywhere, anywhere,
                  pl.BlockSpec(memory_space=pltpu.VMEM), anywhere, anywhere],
        out_specs=[anywhere] * 3,
        scratch_shapes=[
            pltpu.VMEM((rows, HD), BF16),
            pltpu.VMEM((rows, HD), BF16),
            pltpu.VMEM((rows, HD), BF16),
            pltpu.VMEM((HD, rows), BF16),
            pltpu.VMEM((HD, rows), BF16),
            pltpu.VMEM((rows, HD), F32),
            pltpu.VMEM((rows, HD), F32),
            pltpu.VMEM((rows, HD), F32),
            pltpu.VMEM((rows, KEYS), BF16),
            pltpu.VMEM((rows, KEYS), BF16),
            pltpu.VMEM((STEPS, 8, KEYS), jnp.int32),
            pltpu.VMEM((ROWS, HD), jnp.int32),
            pltpu.VMEM((STEPS, KEYS, 2 * HD), BF16),
            pltpu.VMEM((STEPS, 2 * HD, KEYS), F32),
            pltpu.VMEM((STEPS, 2 * HD, KEYS), BF16),
            pltpu.VMEM((8, 2 * HD, KEYS), BF16),
            pltpu.VMEM((6, 2, 2 * HD, STRETCH), BF16),
            pltpu.VMEM((6, 2, 2 * HD, STRETCH), BF16),
            pltpu.VMEM((2 * HD, KEYS), BF16),
            pltpu.VMEM((2 * HD, KEYS), BF16),
            pltpu.VMEM((ROWS, HEADS * HD), BF16),
            pltpu.VMEM((ROWS, HD), BF16),
            pltpu.VMEM((ROWS, HD), BF16),
            pltpu.SemaphoreType.DMA((43,)),
            pltpu.SemaphoreType.DMA((43,)),
            pltpu.SemaphoreType.DMA((14,)),
            pltpu.SemaphoreType.DMA((3,)),
        ],
        compiler_params=pltpu.CompilerParams(
            vmem_limit_bytes=58 * 2**20, collective_id=0, has_side_effects=True
        ),
    )(stretch_order, queries, out_grads, outputs, log_norms, keys, values)
    return pl.pallas_call(
        hand_over,
        out_shape=shapes,
        in_specs=[pl.BlockSpec(memory_space=pltpu.VMEM)] * 3,
        out_specs=[pl.BlockSpec(memory_space=pltpu.VMEM)] * 3,
    )(*grads)


def solution(mesh):
    return jax.shard_map(
        shards,
        mesh=mesh,
        in_specs=(
            PartitionSpec(("dp", "ctx"), "tp"),
            PartitionSpec(("dp", "ctx"), "tp"),
            PartitionSpec(("dp", "ctx"), "tp"),
            PartitionSpec(("dp", "ctx"), "tp"),
            PartitionSpec(("dp", "ctx"), "tp"),
            PartitionSpec("tp", ("dp", "ctx")),
            PartitionSpec("dp"),
        ),
        out_specs=(PartitionSpec(("dp", "ctx"), "tp"), PartitionSpec(("dp", "ctx"), "tp"), PartitionSpec(("dp", "ctx"), "tp")),
        check_vma=False,
    )
```

time: 210 us -> 58.1 us (0.28)
  waiting for transfers between devices: 144 us -> 0 us
  between operations: 13.8 us -> 0.64 us
  Pallas kernels: 47.7 us -> 57.3 us
  local copies, waits for them, and re-layouts: 3.36 us -> 0 us
    all_gather x2 -> x0, waiting for transfers between devices: 72.6 us -> none  [the longest x1 36.9 us: shards(): key_all = lax.all_gather(keys, 'ctx', axis=0, tiled=True)]
    reduce_scatter x1 -> x0, waiting for transfers between devices: 70.2 us -> none  [shards(): summed = lax.psum_scatter(term, 'ctx', scatter_dimension=0, tiled=True)]
    pallas_call x1 -> x2, Pallas kernels: 47.7 us -> 57.3 us  [the longest x1 55.3 us: shards(): pl.pallas_call(kernel, out_shape=shapes, in_specs=[pl.BlockSpec(memory_sp...]
  transfers between devices with their start and end apart: 3 -> 0, of which waited for: 3 -> 0; matrix products, arithmetic and copies ran while one was open for 0% -> 0% of each run, Pallas kernels for 0% -> 0%
where the time goes in v4:
time: 58.1 us; the launch traced here: 57.9 us
  Pallas kernels  57.3 us (99%)
  between operations  0.64 us (1%)
    pallas_call x1, Pallas kernels, shards(): pl.pallas_call(kernel, out_shape=shapes, in_specs=[pl.BlockSpec(memory_sp...  55.3 us
    pallas_call x1, Pallas kernels, shards(): pl.pallas_call(hand_over, out_shape=shapes, in_specs=[pl.BlockSpec(memory...  2.01 us

profile of v4, /device:TPU:0, one launch (start us, length us, event | category | flops | bytes accessed | tf_op | source)
XLA Modules:
  0.0 57.9 jit_solution(1874107240030160419)
XLA Ops:
  0.6 55.3 %shard_map.94 = (bf16[512,512]{1,0:T(8,128)(2,1)}, bf16[512,128]{1,0:T(8,128)(2,1)}, bf16[512,128]{1,0:T(8,128)(2,1)}) custom-call(s32[32]{0:T(128)} %order.1, bf16[512,512]{1,0:T(8,128)(2,1)} %q_in.1, bf16[512,512]{1,0:T(8,128)(2,1)} %do_in.1, bf16[512,512]{1,0:T(8,128)(2,1)} %o_in.1, f32[4,512]{1,0:T(4,128)} %norm_in.1, bf16[512,128]{1,0:T(8,128)(2,1)} %k_in.1, ...), custom_call_target="tpu_custom_call" | custom-call | tf_op jit(solution)/shard_map/pallas_call | solution.py:297
  55.9 2.0 %shard_map.95 = (bf16[512,512]{1,0:T(8,128)(2,1)}, bf16[512,128]{1,0:T(8,128)(2,1)}, bf16[512,128]{1,0:T(8,128)(2,1)}) custom-call(bf16[512,512]{1,0:T(8,128)(2,1)} %get-tuple-element.6.dq, bf16[512,128]{1,0:T(8,128)(2,1)} %get-tuple-element.7.dk, bf16[512,128]{1,0:T(8,128)(2,1)} %get-tuple-element.8.dv), custom_call_target="tpu_custom_call" | custom-call | tf_op jit(solution)/shard_map/pallas_call | solution.py:336

commit v5 on v4

--- a/solution.py
+++ b/solution.py
@@ -101,12 +101,6 @@
     loads = [pltpu.make_async_copy(src, dst, isem.at[n]) for n, (src, dst) in enumerate(loads)]
     for load in loads:
         load.start()
-    loads[0].wait()
-    loads[1].wait()
-    pl.semaphore_wait(barrier, 5)
-    start("ou0 od0 ox0 ou1 od1 ox1 o")
-    dqa[...] = jnp.zeros_like(dqa)
-
     row_iota = lax.broadcasted_iota(jnp.int32, (8, STRETCH), 1)
     col_iota = lax.broadcasted_iota(jnp.int32, (STRETCH, HD), 0)
     other_core = 1 - core
@@ -128,11 +122,19 @@
     for h in range(2):
         qpos[h * STRETCH : (h + 1) * STRETCH] = col_iota + order[me * 2 + h] * STRETCH
 
+    dqa[...] = jnp.zeros_like(dqa)
+    loads[0].wait()
+    loads[1].wait()
+    pl.semaphore_wait(barrier, 5)
+    start("ou0 od0 ox0")
+
     norm = norm_in[...] * LOG2E
     norm_cols = jnp.concatenate([norm, norm], axis=0).T
-    for load in loads[2:]:
-        load.wait()
     for h in range(HEADS):
+        for load in loads[2 + 3 * h : 5 + 3 * h]:
+            load.wait()
+        if h == 2:
+            start("ou1 od1 ox1 o")
         rows = slice(h * ROWS, (h + 1) * ROWS)
         do = doh[rows, :]
         qt[:, rows] = qh[rows, :].T
@@ -258,32 +260,43 @@
         dqb[:, cols] = (dqa[h * ROWS : (h + 1) * ROWS, :] * SCALE).astype(BF16)
     outs.append(pltpu.make_async_copy(dqb, dq_out, osem.at[0]))
     outs[0].start()
-    arrived("os pu0 pd0 pu1 pd1")
+    arrived("os")
+    arrived("pu0 pd0 pu1 pd1")
     for h in range(2):
         cols = slice(h * STRETCH, (h + 1) * STRETCH)
         acc[O, :, cols] += (r_sib[0, :, cols].astype(F32) + r_in[h, 0].astype(F32)
                             + r_in[h, 1].astype(F32))
-    arrived("qx0 qz0")
-    acc[O, :, 0:STRETCH] += r_in[4, 0].astype(F32) + r_in[4, 1].astype(F32)
-    arrived("qx1 qz1")
-    acc[O, :, STRETCH:] += r_in[5, 0].astype(F32) + r_in[5, 1].astype(F32)
-    total = acc[O]
-    dkb[...] = (total[0:HD] * SCALE).astype(BF16).T
-    dvb[...] = total[HD:].astype(BF16).T
-    outs.append(pltpu.make_async_copy(dkb, dk_out, osem.at[1]))
-    outs.append(pltpu.make_async_copy(dvb, dv_out, osem.at[2]))
-    outs[1].start()
-    outs[2].start()
+    for h in range(2):
+        cols = slice(h * STRETCH, (h + 1) * STRETCH)
+        arrived(f"qx{h} qz{h}")
+        total = acc[O, :, cols] + r_in[4 + h, 0].astype(F32) + r_in[4 + h, 1].astype(F32)
+        dkb[cols, :] = (total[0:HD] * SCALE).astype(BF16).T
+        dvb[cols, :] = total[HD:].astype(BF16).T
+        for n, (src, dst) in enumerate(((dkb, dk_out), (dvb, dv_out))):
+            out = pltpu.make_async_copy(src.at[HALVES[h]], dst.at[HALVES[h]],
+                                        osem.at[1 + 2 * h + n])
+            out.start()
+            outs.append(out)
     for name in copies:
         copy(number[name], *copies[name]).wait_send()
     for out in outs:
         out.wait()
 
 
-def hand_over(dq, dk, dv, dq_out, dk_out, dv_out):
-    dq_out[...] = dq[...]
-    dk_out[...] = dk[...]
-    dv_out[...] = dv[...]
+def hand_over(dq, dk, dv, dq_out, dk_out, dv_out, dqb, dkb, dvb, sem_in, sem_out):
+    moves = []
+    for n, refs in enumerate(((dq, dqb, dq_out), (dk, dkb, dk_out), (dv, dvb, dv_out))):
+        for h in range(2):
+            src, mid, dst = (ref.at[HALVES[h]] for ref in refs)
+            moves.append((pltpu.make_async_copy(src, mid, sem_in.at[2 * n + h]),
+                          pltpu.make_async_copy(mid, dst, sem_out.at[2 * n + h])))
+    for load, _ in moves:
+        load.start()
+    for load, store in moves:
+        load.wait()
+        store.start()
+    for _, store in moves:
+        store.wait()
 
 
 def shards(queries, keys, values, outputs, out_grads, log_norms, stretch_order):
@@ -327,7 +340,7 @@
             pltpu.SemaphoreType.DMA((43,)),
             pltpu.SemaphoreType.DMA((43,)),
             pltpu.SemaphoreType.DMA((14,)),
-            pltpu.SemaphoreType.DMA((3,)),
+            pltpu.SemaphoreType.DMA((5,)),
         ],
         compiler_params=pltpu.CompilerParams(
             vmem_limit_bytes=58 * 2**20, collective_id=0, has_side_effects=True
@@ -336,8 +349,10 @@
     return pl.pallas_call(
         hand_over,
         out_shape=shapes,
-        in_specs=[pl.BlockSpec(memory_space=pltpu.VMEM)] * 3,
-        out_specs=[pl.BlockSpec(memory_space=pltpu.VMEM)] * 3,
+        in_specs=[anywhere] * 3,
+        out_specs=[anywhere] * 3,
+        scratch_shapes=[pltpu.VMEM(shape.shape, BF16) for shape in shapes]
+        + [pltpu.SemaphoreType.DMA((6,)), pltpu.SemaphoreType.DMA((6,))],
     )(*grads)
 
 

time: 58.1 us -> 58 us (level)
  no operation moved by 1% of the time
where the time goes in v5:
time: 58 us; the launch traced here: 57.8 us
  Pallas kernels  57.1 us (98%)
  between operations  0.64 us (1%)
    pallas_call x1, Pallas kernels, shards(): pl.pallas_call(kernel, out_shape=shapes, in_specs=[pl.BlockSpec(memory_sp...  55.2 us
    pallas_call x1, Pallas kernels, shards(): pl.pallas_call(hand_over, out_shape=shapes, in_specs=[anywhere] * 3, out_...  1.92 us

profile of v5, /device:TPU:0, one launch (start us, length us, event | category | flops | bytes accessed | tf_op | source)
XLA Modules:
  0.0 57.8 jit_solution(9408807501738005861)
XLA Ops:
  0.6 55.2 %shard_map.94 = (bf16[512,512]{1,0:T(8,128)(2,1)}, bf16[512,128]{1,0:T(8,128)(2,1)}, bf16[512,128]{1,0:T(8,128)(2,1)}) custom-call(s32[32]{0:T(128)} %order.1, bf16[512,512]{1,0:T(8,128)(2,1)} %q_in.1, bf16[512,512]{1,0:T(8,128)(2,1)} %do_in.1, bf16[512,512]{1,0:T(8,128)(2,1)} %o_in.1, f32[4,512]{1,0:T(4,128)} %norm_in.1, bf16[512,128]{1,0:T(8,128)(2,1)} %k_in.1, ...), custom_call_target="tpu_custom_call" | custom-call | tf_op jit(solution)/shard_map/pallas_call | solution.py:310
  55.9 1.9 %shard_map.95 = (bf16[512,512]{1,0:T(8,128)(2,1)}, bf16[512,128]{1,0:T(8,128)(2,1)}, bf16[512,128]{1,0:T(8,128)(2,1)}) custom-call(bf16[512,512]{1,0:T(8,128)(2,1)} %get-tuple-element.6.dq, bf16[512,128]{1,0:T(8,128)(2,1)} %get-tuple-element.7.dk, bf16[512,128]{1,0:T(8,128)(2,1)} %get-tuple-element.8.dv), custom_call_target="tpu_custom_call" | custom-call | tf_op jit(solution)/shard_map/pallas_call | solution.py:349

commit v6 on v5

--- a/solution.py
+++ b/solution.py
@@ -184,10 +184,10 @@
             arrived("ou0 od0")
             start("z0 p0")
             arrived("ox0")
-            start("xd0")
+            start("xd0 xu0")
         if t == P1:
             arrived("ou1 od1")
-            start("z1 xu0 p1")
+            start("z1 p1")
         if t == P0S:
             arrived("ox1")
             start("xu1 xd1")

time: 58 us -> 58 us (level)
  no operation moved by 1% of the time
where the time goes in v6:
time: 58 us; the launch traced here: 57.8 us
  Pallas kernels  57.1 us (98%)
  between operations  0.64 us (1%)
    pallas_call x1, Pallas kernels, shards(): pl.pallas_call(kernel, out_shape=shapes, in_specs=[pl.BlockSpec(memory_sp...  55.2 us
    pallas_call x1, Pallas kernels, shards(): pl.pallas_call(hand_over, out_shape=shapes, in_specs=[anywhere] * 3, out_...  1.92 us

profile of v6, /device:TPU:0, one launch (start us, length us, event | category | flops | bytes accessed | tf_op | source)
XLA Modules:
  0.0 57.8 jit_solution(9417662849215186788)
XLA Ops:
  0.6 55.2 %shard_map.94 = (bf16[512,512]{1,0:T(8,128)(2,1)}, bf16[512,128]{1,0:T(8,128)(2,1)}, bf16[512,128]{1,0:T(8,128)(2,1)}) custom-call(s32[32]{0:T(128)} %order.1, bf16[512,512]{1,0:T(8,128)(2,1)} %q_in.1, bf16[512,512]{1,0:T(8,128)(2,1)} %do_in.1, bf16[512,512]{1,0:T(8,128)(2,1)} %o_in.1, f32[4,512]{1,0:T(4,128)} %norm_in.1, bf16[512,128]{1,0:T(8,128)(2,1)} %k_in.1, ...), custom_call_target="tpu_custom_call" | custom-call | tf_op jit(solution)/shard_map/pallas_call | solution.py:310
  55.9 1.9 %shard_map.95 = (bf16[512,512]{1,0:T(8,128)(2,1)}, bf16[512,128]{1,0:T(8,128)(2,1)}, bf16[512,128]{1,0:T(8,128)(2,1)}) custom-call(bf16[512,512]{1,0:T(8,128)(2,1)} %get-tuple-element.6.dq, bf16[512,128]{1,0:T(8,128)(2,1)} %get-tuple-element.7.dk, bf16[512,128]{1,0:T(8,128)(2,1)} %get-tuple-element.8.dv), custom_call_target="tpu_custom_call" | custom-call | tf_op jit(solution)/shard_map/pallas_call | solution.py:349
